TPU v7x, 32 devices: a whole 2x2x4 slice. The times are simulated.
32 devices in a mesh: emb: 16 (over z, y, x), dp: 2 (over core).
Axes of the slice: x: 2, y: 2, z: 4, core: 2. Of those that a mesh axis runs over, the one named last changes fastest.
Arguments:
- hashed_ids: int32 [256, 128], P(('emb', 'dp')), may hold values from 0 to 8191
- owners: int32 [256, 128, 1], P(('emb', 'dp')), may hold values from 0 to 15; in each aligned block of 1024 rows (0 to 1023, 1024 to 2047, ..., all dimensions but the last counted through in order) at most 128 rows name the same one
- domain_tags: int32 [256], P(('emb', 'dp')), may hold values from 0 to 2
- user_counts: int32 [3], replicated, may hold values from 512 to 8192
- lengths: int32 [32, 8], P(('emb', 'dp')), may hold values from 1 to 128, 640 in all within a row
- buckets: int32 [128, 128], replicated, may hold values from 0 to 31
- table: bfloat16 [524288, 128], P('emb'), may hold values from -6 to 6
- gain_one: float32 [128], replicated, may hold values from 0.5 to 1.5
- query_weight_matrix: bfloat16 [128, 384], replicated, may hold values from -0.5 to 0.5
- key_weight_matrix: bfloat16 [128, 384], replicated, may hold values from -0.5 to 0.5
- value_weight_matrix: bfloat16 [128, 384], replicated, may hold values from -0.5 to 0.5
- attention_output_weight: bfloat16 [384, 128], replicated, may hold values from -0.875 to 0.875
- bias_table: float32 [32, 6], replicated, may hold values from -4 to 4
- gain_two: float32 [128], replicated, may hold values from 0.5 to 1.5
- feedforward_input_weight: bfloat16 [128, 1024], replicated, may hold values from -0.5 to 0.5
- feedforward_output_weight: bfloat16 [1024, 128], replicated, may hold values from -0.1875 to 0.1875
- cotangent: bfloat16 [256, 128, 128], P(('emb', 'dp')), may hold values from -6 to 6
Outputs:
- output: bfloat16 [256, 128, 128], P(('emb', 'dp'))
- input_grad: float32 [256, 128, 128], P(('emb', 'dp'))
- table_grad: float32 [524288, 128], P('emb')
- gain_one_grad: float32 [128], replicated
- w_query_grad: float32 [128, 384], replicated
- w_key_grad: float32 [128, 384], replicated
- w_value_grad: float32 [128, 384], replicated
- w_output_grad: float32 [384, 128], replicated
- bias_grad: float32 [32, 6], replicated
- gain_two_grad: float32 [128], replicated
- w_in_grad: float32 [128, 1024], replicated
- w_out_grad: float32 [1024, 128], replicated
Inputs may be any that keep to these rules, and one draw needn't show every extreme that they name: `owners`: among the 1024 tokens of one device no shard is named more than 128 times, and in some device's tokens one shard is named exactly 128 times. The 8 lengths of each row sum to 640 and the largest of each row is 128.
All inputs are finite; a program needn't handle non-finite values.
Results may differ from a plain program's by a relative error of at most 0.012.
Values may be sent and summed in bfloat16 or wider, within the bound.
A program may use at most 128 MiB of HBM per device.

v0:
```python
import functools
import math

import jax
import jax.numpy as jnp
from jax import lax
from jax.experimental import pallas as pl
from jax.experimental.pallas import tpu as pltpu
from jax.sharding import PartitionSpec as P

DH = 64
LANES = 128
EPSILON = 1e-06
MESH = pl.DeviceIdType.MESH
F32 = jnp.float32
BF16 = jnp.bfloat16
VMEM_LIMIT = 60 * 1024 * 1024


def dot_nn(a, b):
    return lax.dot_general(a, b, (((1,), (0,)), ((), ())), preferred_element_type=F32)


def dot_nt(a, b):
    return lax.dot_general(a, b, (((1,), (1,)), ((), ())), preferred_element_type=F32)


def dot_tn(a, b):
    return lax.dot_general(a, b, (((0,), (0,)), ((), ())), preferred_element_type=F32)


def hot_slots(pos, first, count):
    rows = lax.broadcasted_iota(jnp.int32, (count, LANES), 0) + first
    parts = [
        jnp.where(rows == pos[s : s + 1, :], 1.0, 0.0).astype(BF16) for s in range(pos.shape[0])
    ]
    return jnp.concatenate(parts, axis=1)


def remote(src, dst, send_sem, recv_sem, device):
    return pltpu.make_async_remote_copy(
        src_ref=src, dst_ref=dst, send_sem=send_sem, recv_sem=recv_sem,
        device_id=device, device_id_type=MESH,
    )


def gelu_parts(u):
    k0 = math.sqrt(2.0 / math.pi)
    k1 = k0 * 0.044715
    square = u * u
    half = 0.5 * jnp.tanh(u * (k1 * square + k0)) + 0.5
    value = u * half
    slope = half + (2.0 * value) * (1.0 - half) * (3.0 * k1 * square + k0)
    return value, slope


def split_pair(both):
    zero = jnp.zeros((DH, LANES), both.dtype)
    left = jnp.concatenate([both[:DH], zero], axis=0)
    right = jnp.concatenate([zero, both[DH:]], axis=0)
    return jnp.concatenate([left, right], axis=1)


class Reducer:
    def __init__(self, n, lo, me, core, part, total, bufs):
        self.n, self.lo, self.hi, self.core = n, lo, n // lo, core
        self.my_hi, self.my_lo = me // lo, lax.rem(me, lo)
        self.part, self.total = part, total
        (
            self.core_buf, self.half, self.lo_buf, self.quarter, self.hi_buf, self.core_sem,
            self.lo_sem, self.hi_sem, self.gh_sem, self.gl_sem, self.gc_sem,
        ) = bufs
        self.half_rows, self.lo_rows = self.half.shape[0], self.quarter.shape[0]
        self.hi_rows = self.hi_buf.shape[1]

    @staticmethod
    def scratch(n, lo, rows):
        hi, dma, width = n // lo, pltpu.SemaphoreType.DMA, LANES
        return [
            pltpu.VMEM((rows // 2, width), BF16),
            pltpu.VMEM((rows // 2, width), BF16),
            pltpu.VMEM((lo, rows // 2 // lo, width), BF16),
            pltpu.VMEM((rows // 2 // lo, width), BF16),
            pltpu.VMEM((hi, rows // 2 // n, width), BF16),
            dma((2,)), dma((2, lo)), dma((2, hi)), dma((2, hi)), dma((2, lo)), dma((2, lo)),
        ]

    def lo_device(self, k):
        return {"emb": self.my_hi * self.lo + self.lo_peer(k)}

    def hi_device(self, k):
        return {"emb": self.hi_peer(k) * self.lo + self.my_lo}

    def lo_peer(self, k):
        return lax.rem(self.my_lo + k, self.lo)

    def hi_peer(self, k):
        return lax.rem(self.my_hi + k, self.hi)

    def swap(self):
        at = pl.ds(pl.multiple_of((1 - self.core) * self.half_rows, self.half_rows), self.half_rows)
        return remote(
            self.part.at[at], self.core_buf, self.core_sem.at[0], self.core_sem.at[1],
            {"dp": 1 - self.core},
        )

    def lo_copy(self, k):
        at = pl.ds(pl.multiple_of(self.lo_peer(k) * self.lo_rows, self.lo_rows), self.lo_rows)
        return remote(
            self.half.at[at], self.lo_buf.at[self.lo - k],
            self.lo_sem.at[0, k], self.lo_sem.at[1, self.lo - k], self.lo_device(k),
        )

    def lo_arrival(self, k):
        return remote(
            self.quarter, self.lo_buf.at[k],
            self.lo_sem.at[0, k], self.lo_sem.at[1, k], self.lo_device(k),
        )

    def hi_copy(self, k):
        at = pl.ds(pl.multiple_of(self.hi_peer(k) * self.hi_rows, self.hi_rows), self.hi_rows)
        return remote(
            self.quarter.at[at], self.hi_buf.at[self.hi - k],
            self.hi_sem.at[0, k], self.hi_sem.at[1, self.hi - k], self.hi_device(k),
        )

    def hi_arrival(self, k):
        return remote(
            self.hi_buf.at[k], self.hi_buf.at[k],
            self.hi_sem.at[0, k], self.hi_sem.at[1, k], self.hi_device(k),
        )

    def piece(self, h):
        at = self.core * self.half_rows + self.my_lo * self.lo_rows + h * self.hi_rows
        return self.total.at[pl.ds(pl.multiple_of(at, self.hi_rows), self.hi_rows)]

    def block(self, core, low):
        at = core * self.half_rows + low * self.lo_rows
        return self.total.at[pl.ds(pl.multiple_of(at, self.lo_rows), self.lo_rows)]

    def gather_hi(self, k):
        mine = self.piece(self.my_hi)
        return remote(
            mine, mine, self.gh_sem.at[0, k], self.gh_sem.at[1, self.hi - k], self.hi_device(k)
        )

    def gather_hi_arrival(self, k):
        other = self.piece(self.hi_peer(k))
        return remote(other, other, self.gh_sem.at[0, k], self.gh_sem.at[1, k], self.hi_device(k))

    def gather_lo(self, k):
        mine = self.block(self.core, self.my_lo)
        return remote(
            mine, mine, self.gl_sem.at[0, k], self.gl_sem.at[1, self.lo - k], self.lo_device(k)
        )

    def gather_lo_arrival(self, k):
        other = self.block(self.core, self.lo_peer(k))
        return remote(other, other, self.gl_sem.at[0, k], self.gl_sem.at[1, k], self.lo_device(k))

    def gather_core(self, low):
        mine = self.block(self.core, low)
        return remote(
            mine, mine, self.gc_sem.at[0, low], self.gc_sem.at[1, low], {"dp": 1 - self.core}
        )

    def gather_core_arrival(self, low):
        other = self.block(1 - self.core, low)
        return remote(
            other, other, self.gc_sem.at[0, low], self.gc_sem.at[1, low], {"dp": 1 - self.core}
        )

    def start(self):
        self.swap().start()

    def core_to_lo(self):
        self.swap().wait()
        step = self.hi_rows

        def add(r, carry):
            at = pl.multiple_of(r * step, step)
            own = self.part[pl.ds(pl.multiple_of(self.core * self.half_rows + at, step), step), :]
            other = self.core_buf[pl.ds(at, step), :]
            self.half[pl.ds(at, step), :] = (own.astype(F32) + other.astype(F32)).astype(BF16)
            return carry

        lax.fori_loop(0, self.half_rows // step, add, 0)
        for k in range(1, self.lo):
            self.lo_copy(k).start()

    def lo_to_hi(self):
        for k in range(1, self.lo):
            self.lo_arrival(k).wait_recv()
        step = self.hi_rows

        def add(r, carry):
            at = pl.multiple_of(r * step, step)
            mine = pl.ds(pl.multiple_of(self.my_lo * self.lo_rows + at, step), step)
            total = self.half[mine, :].astype(F32)
            for k in range(1, self.lo):
                total = total + self.lo_buf[k, pl.ds(at, step), :].astype(F32)
            self.quarter[pl.ds(at, step), :] = total.astype(BF16)
            return carry

        lax.fori_loop(0, self.lo_rows // step, add, 0)
        for k in range(1, self.hi):
            self.hi_copy(k).start()

    def hi_to_gather(self):
        for k in range(1, self.hi):
            self.hi_arrival(k).wait_recv()
        mine = pl.ds(pl.multiple_of(self.my_hi * self.hi_rows, self.hi_rows), self.hi_rows)
        total = self.quarter[mine, :].astype(F32)
        for k in range(1, self.hi):
            total = total + self.hi_buf[k].astype(F32)
        self.piece(self.my_hi)[...] = total.astype(BF16)
        for k in range(1, self.hi):
            self.gather_hi(k).start()

    def gather_to_lo(self):
        for k in range(1, self.hi):
            self.gather_hi_arrival(k).wait_recv()
        for k in range(1, self.lo):
            self.gather_lo(k).start()
        self.gather_core(self.my_lo).start()

    def gather_to_core(self):
        for k in range(1, self.lo):
            self.gather_lo_arrival(k).wait_recv()
            self.gather_core(self.lo_peer(k)).start()

    def finish(self):
        for low in range(self.lo):
            self.gather_core_arrival(low).wait_recv()
        for k in range(1, self.lo):
            self.lo_copy(k).wait_send()
            self.gather_lo(k).wait_send()
        for k in range(1, self.hi):
            self.hi_copy(k).wait_send()
            self.gather_hi(k).wait_send()
        for low in range(self.lo):
            self.gather_core(low).wait_send()


class SmallReducer:
    def __init__(self, n, lo, me, core, total, bufs):
        self.lo, self.hi, self.core = lo, n // lo, core
        self.my_hi, self.my_lo = me // lo, lax.rem(me, lo)
        self.total = total
        self.a, self.b, self.c, self.a_sem, self.b_sem, self.c_sem = bufs

    @staticmethod
    def scratch(n, lo):
        hi, dma = n // lo, pltpu.SemaphoreType.DMA
        return [
            pltpu.VMEM((2, 8, LANES), F32),
            pltpu.VMEM((lo, 8, LANES), F32),
            pltpu.VMEM((hi, 8, LANES), F32),
            dma((2,)), dma((2, lo)), dma((2, hi)),
        ]

    def swap(self, slot):
        ref = self.a.at[slot]
        return remote(ref, ref, self.a_sem.at[0], self.a_sem.at[1], {"dp": 1 - self.core})

    def lo_copy(self, k, slot, come):
        device = {"emb": self.my_hi * self.lo + lax.rem(self.my_lo + k, self.lo)}
        ref = self.b.at[slot]
        return remote(ref, ref, self.b_sem.at[0, k], self.b_sem.at[1, come], device)

    def hi_copy(self, k, slot, come):
        device = {"emb": lax.rem(self.my_hi + k, self.hi) * self.lo + self.my_lo}
        ref = self.c.at[slot]
        return remote(ref, ref, self.c_sem.at[0, k], self.c_sem.at[1, come], device)

    def start(self, value):
        self.a[self.core] = value
        self.swap(self.core).start()

    def core_to_lo(self):
        self.swap(self.core).wait_send()
        self.swap(1 - self.core).wait_recv()
        self.b[self.my_lo] = self.a[0] + self.a[1]
        for k in range(1, self.lo):
            self.lo_copy(k, self.my_lo, self.lo - k).start()

    def lo_to_hi(self):
        for k in range(1, self.lo):
            self.lo_copy(k, lax.rem(self.my_lo + k, self.lo), k).wait_recv()
        total = self.b[0]
        for k in range(1, self.lo):
            total = total + self.b[k]
        self.c[self.my_hi] = total
        for k in range(1, self.hi):
            self.hi_copy(k, self.my_hi, self.hi - k).start()

    def finish(self):
        for k in range(1, self.hi):
            self.hi_copy(k, lax.rem(self.my_hi + k, self.hi), k).wait_recv()
        total = self.c[0]
        for k in range(1, self.hi):
            total = total + self.c[k]
        self.total[...] = total
        for k in range(1, self.lo):
            self.lo_copy(k, self.my_lo, self.lo - k).wait_send()
        for k in range(1, self.hi):
            self.hi_copy(k, self.my_hi, self.hi - k).wait_send()


def step_body(
    n, lo, cap, used, refs_in, refs_out, lookup_refs, block_refs, early_refs, late_refs, small_refs,
):
    (
        ids_far, own_far, tags_far, counts_far, lens_far, btab_far, buckets_far, g1_far, g2_far,
        table, *far,
    ) = refs_in
    y_far, ig_far, inc, asked_far, early_far, late_far, small_far = refs_out
    (
        req, asked_v, asked_s, tab_low, tab, gbuf, send, recv, x_acc, pos_ref, slots, early, late,
        back_pos, back_req, back_send, back_recv,
        req_send, req_recv, row_send, row_recv, pair_sem, tab_sem, smem_sem,
        grad_send, grad_recv, fwd_send, fwd_recv,
    ) = lookup_refs
    (
        wqkv_t, wqkv, wo_t, win_t, wout_t, buck_t, bias, x_t, a_t, qkv_t, kv, p_s, o_t, c_t, act_t,
        du_t, dy_t, dm_t, dmb_t, do_t, dqkv_t, dsum, igb_t, b_acc,
        cot, wq, wk, wv, wo, win, wout, near_sem,
        ids, own, tags, counts, lens, btab, buckets, g1, g2, first_sem,
        y_out, ig_out, asked_out, early_tot, late_tot, small_tot, out_sem,
    ) = block_refs
    near = (cot, wq, wk, wv, wo, win, wout, btab, buckets, g1, g2)
    far = tuple(far) + (btab_far, buckets_far, g1_far, g2_far)
    me = lax.axis_index("emb")
    core = lax.axis_index("dp")
    seqs, length = ids.shape
    width = cot.shape[2]
    tokens = seqs * length
    hd, ff = wq.shape[1], win.shape[1]
    heads = hd // DH
    pairs = heads // 2
    bucket_count = btab.shape[1]
    domain_rows = used // 3
    row_limit = 4 * domain_rows
    pieces = tab_sem.shape[0]
    piece = used // pieces
    group = 4
    wide_slots = 256
    early_sum = Reducer(n, lo, me, core, early, early_tot, early_refs)
    late_sum = Reducer(n, lo, me, core, late, late_tot, late_refs)
    small_sum = SmallReducer(n, lo, me, core, small_tot, small_refs)

    barrier = pltpu.get_barrier_semaphore()

    def peer(j):
        return {"emb": lax.rem(me + j, n)}

    def greet(k, carry):
        pl.semaphore_signal(barrier, inc=1, device_id=peer(k), device_id_type=MESH)
        return carry

    lax.fori_loop(1, n, greet, 0)
    pl.semaphore_signal(barrier, inc=1, device_id={"dp": 1 - core}, device_id_type=MESH)
    first = [
        pltpu.make_async_copy(src, dst, first_sem.at[k])
        for k, (src, dst) in enumerate(
            (
                (ids_far, ids), (own_far, own), (tags_far, tags), (counts_far, counts),
                (lens_far, lens),
            )
        )
    ]
    for fetch in first:
        fetch.start()

    def table_copy(c):
        part = pl.ds(c * piece, piece)
        return pltpu.make_async_copy(table.at[part], tab_low.at[part], tab_sem.at[c])

    for c in range(pieces):
        table_copy(c).start()
    fetches = [
        pltpu.make_async_copy(src, dst, near_sem.at[k])
        for k, (src, dst) in enumerate(zip(far, near))
    ]
    for fetch in fetches:
        fetch.start()

    for fetch in first:
        fetch.wait()

    row_id = lax.broadcasted_iota(jnp.int32, (seqs, length), 0)
    lane_id = lax.broadcasted_iota(jnp.int32, (seqs, length), 1)
    count_of = jnp.ones((seqs, length), F32)
    tag_of = jnp.zeros((seqs, length), jnp.int32)
    len_of = jnp.zeros((seqs, length), jnp.int32)
    for s in range(seqs):
        tag = tags[s]
        count_of = jnp.where(row_id == s, counts[tag].astype(F32), count_of)
        tag_of = jnp.where(row_id == s, tag, tag_of)
        len_of = jnp.where(row_id == s, lens[0, s], len_of)
    code = ids[...].astype(F32)
    turns = jnp.floor((code + 0.5) / jnp.maximum(count_of, 1.0))
    local = tag_of * domain_rows + (code - turns * count_of).astype(jnp.int32)
    live = lane_id < len_of
    rel = own[...] - me
    rel = jnp.where(rel < 0, rel + n, rel)

    owner_id = lax.broadcasted_iota(jnp.int32, (n, length), 0)
    hots = [jnp.where(owner_id == rel[s : s + 1, :], 1.0, 0.0) for s in range(seqs)]
    before = (
        lax.broadcasted_iota(jnp.int32, (length, length), 0)
        < lax.broadcasted_iota(jnp.int32, (length, length), 1)
    )
    earlier = jnp.where(before, 1.0, 0.0).astype(BF16)
    prefix = dot_nn(jnp.concatenate(hots, axis=0).astype(BF16), earlier)
    running = jnp.zeros((n, 1), F32)
    ranks = []
    for s in range(seqs):
        ranks.append(
            jnp.sum(hots[s] * (prefix[s * n : s * n + n] + running), axis=0, keepdims=True)
        )
        running = running + jnp.sum(hots[s], axis=1, keepdims=True)
    rank = jnp.concatenate(ranks, axis=0).astype(jnp.int32)
    pos_ref[...] = rel * cap + rank

    low = (local & 255).astype(F32)
    high = lax.shift_right_logical(local, 8).astype(F32)
    slot_id = lax.broadcasted_iota(jnp.int32, (LANES, length), 0)
    asking = jnp.zeros((2 * n, LANES), F32)
    for s in range(seqs):
        hot = hots[s]
        values = jnp.concatenate([hot * high[s : s + 1, :], hot * low[s : s + 1, :]], axis=0)
        slot_hot = jnp.where(slot_id == rank[s : s + 1, :], 1.0, 0.0).astype(BF16)
        asking = asking + dot_nt(values.astype(BF16), slot_hot)
    wanted = (asking[:n] * 256.0 + asking[n:]).astype(jnp.int32)
    for j in range(n):
        req[j] = wanted[j : j + 1, :]

    pl.semaphore_wait(barrier, n)

    def request(j):
        back = lax.rem(n - j, n)
        return remote(req.at[j], asked_v.at[back], req_send.at[j], req_recv.at[back], peer(j))

    def request_arrival(j):
        return remote(req.at[j], asked_v.at[j], req_send.at[j], req_recv.at[j], peer(j))

    def ask(j, carry):
        request(j).start()
        return carry

    lax.fori_loop(1, n, ask, 0)
    asked_v[0] = req[0]

    for c in range(pieces):
        table_copy(c).wait()

        def widen(r, carry):
            part = pl.ds(pl.multiple_of(c * piece + r * 256, 256), 256)
            tab[part, :] = tab_low[part, :].astype(F32)
            return carry

        lax.fori_loop(0, piece // 256, widen, 0)

    def all_asked(j, carry):
        request_arrival(j).wait_recv()
        return carry

    lax.fori_loop(1, n, all_asked, 0)
    to_scalar = pltpu.make_async_copy(asked_v, asked_s, smem_sem)
    to_scalar.start()
    to_scalar.wait()

    def slot_block(j):
        return pl.ds(pl.multiple_of(j * cap, cap), cap)

    def row_copy(j):
        back = lax.rem(n - j, n)
        return remote(
            send.at[slot_block(j)], recv.at[slot_block(back)],
            row_send.at[j], row_recv.at[back], peer(j),
        )

    def row_arrival(j):
        at = slot_block(j)
        return remote(send.at[at], recv.at[at], row_send.at[j], row_recv.at[j], peer(j))

    def gather(j):
        def some(c, carry):
            for r in range(16):
                at = asked_s[j, 0, c * 16 + r] & (row_limit - 1)
                gbuf[pl.ds(c * 16 + r, 1), :] = tab[pl.ds(at, 1), :]
            return carry

        lax.fori_loop(0, cap // 16, some, 0)
        return gbuf[...].astype(BF16)

    def pair_at(step):
        half = (step + 1) // 2
        return jnp.where(lax.rem(step, 2) == 1, n // 4 - half, n // 4 + half)

    def serve(step, carry):
        def one(j, inner):
            send[slot_block(j), :] = gather(j)
            row_copy(j).start()
            return inner

        last = n - 2 * pair_at(step)
        return lax.fori_loop(last - 1, jnp.minimum(last + 1, n), one, carry)

    lax.fori_loop(0, n // 2, serve, 0)
    recv[0:cap, :] = gather(0)

    key = jnp.where(live, (rel * row_limit + local).astype(F32), -1.0)
    key_cols = [
        jnp.broadcast_to(key[s : s + 1, :], (length, length)).T for s in range(seqs)
    ]
    fresh = []
    for s in range(seqs):
        seen = jnp.where(before & (key_cols[s] == key[s : s + 1, :]), 1.0, 0.0)
        for e in range(s):
            seen = jnp.maximum(seen, jnp.where(key_cols[e] == key[s : s + 1, :], 1.0, 0.0))
        fresh.append(1.0 - jnp.max(seen, axis=0, keepdims=True))
    fresh = [jnp.where(live[s : s + 1, :], fresh[s], 0.0) for s in range(seqs)]
    news = [hots[s] * fresh[s] for s in range(seqs)]
    prefix = dot_nn(jnp.concatenate(news, axis=0).astype(BF16), earlier)
    running = jnp.zeros((n, 1), F32)
    firsts = []
    for s in range(seqs):
        firsts.append(
            jnp.sum(news[s] * (prefix[s * n : s * n + n] + running), axis=0, keepdims=True)
        )
        running = running + jnp.sum(news[s], axis=1, keepdims=True)
    first_cols = [
        jnp.broadcast_to(firsts[s] * fresh[s] + fresh[s], (length, length)).T for s in range(seqs)
    ]
    found = []
    for s in range(seqs):
        at = jnp.zeros((length, length), F32)
        for e in range(s + 1):
            at = jnp.maximum(at, jnp.where(key_cols[e] == key[s : s + 1, :], first_cols[e], 0.0))
        found.append(jnp.max(at, axis=0, keepdims=True))
    found = jnp.concatenate(found, axis=0).astype(jnp.int32) - 1
    back_pos[...] = jnp.where(live, rel * cap + found, -1)
    below = used - local
    low = (below & 255).astype(F32)
    high = lax.shift_right_logical(below, 8).astype(F32)
    asking = jnp.zeros((2 * n, LANES), F32)
    for s in range(seqs):
        values = jnp.concatenate(
            [news[s] * high[s : s + 1, :], news[s] * low[s : s + 1, :]], axis=0
        )
        slot_hot = jnp.where(slot_id == firsts[s].astype(jnp.int32), 1.0, 0.0).astype(BF16)
        asking = asking + dot_nt(values.astype(BF16), slot_hot)
    wanted = used - (asking[:n] * 256.0 + asking[n:]).astype(jnp.int32)
    limits = jnp.broadcast_to(running, (n, LANES)).astype(jnp.int32)
    for j in range(n):
        back_req[j, 0:1] = wanted[j : j + 1, :]
        back_req[j, 1:2] = limits[j : j + 1, :]
    asked_out[core, 0] = back_req[0]

    def back_request(j):
        back = lax.rem(n - j, n)
        return remote(
            back_req.at[j], asked_out.at[core, back], back_send.at[j], back_recv.at[back], peer(j)
        )

    def back_request_arrival(j):
        return remote(
            back_req.at[j], asked_out.at[core, j], back_send.at[j], back_recv.at[j], peer(j)
        )

    def tell(j, carry):
        back_request(j).start()
        return carry

    lax.fori_loop(1, n, tell, 0)

    def share(which):
        ref = asked_out.at[which]
        return remote(ref, ref, pair_sem.at[0], pair_sem.at[1], {"dp": 1 - core})

    for fetch in fetches:
        fetch.wait()
    for part, w in enumerate((wq, wk, wv)):
        wqkv[:, part * hd : (part + 1) * hd] = w[...]
        wqkv_t[part * hd : (part + 1) * hd, :] = w[...].T
    wo_t[...] = wo[...].T
    win_t[...] = win[...].T
    wout_t[...] = wout[...].T
    buck_t[...] = buckets[...].astype(F32).T
    g1_col = jnp.broadcast_to(g1[...], (8, width)).T[:, 0:1]
    g2_col = jnp.broadcast_to(g2[...], (8, width)).T[:, 0:1]
    dsum[...] = jnp.zeros_like(dsum)
    b_acc[...] = jnp.zeros_like(b_acc)

    def bias_rows(r, carry):
        part = pl.ds(pl.multiple_of(r * 8, 8), 8)
        bt = buck_t[part, :]
        rows = [jnp.zeros((8, length), F32) for _ in range(heads)]
        for b in range(bucket_count):
            here = bt == float(b)
            rows = [jnp.where(here, btab[h, b], rows[h]) for h in range(heads)]
        for p in range(pairs):
            bias[p, part, :] = jnp.concatenate(rows[2 * p : 2 * p + 2], axis=1)
        return carry

    lax.fori_loop(0, length // 8, bias_rows, 0)

    def load_dy(s, carry):
        part = pl.ds(pl.multiple_of(s * length, length), length)
        alive = lax.broadcasted_iota(jnp.int32, (width, length), 1) < lens[0, s]
        dy_t[:, part] = jnp.where(alive, cot[s].astype(F32).T, 0.0).astype(BF16)
        return carry

    lax.fori_loop(0, seqs, load_dy, 0)

    def place(step, carry):
        pair = pair_at(step)

        def ready(j, inner):
            row_arrival(j).wait_recv()
            return inner

        lax.fori_loop(jnp.maximum(2 * pair, 1), 2 * pair + 2, ready, 0)
        first = pl.multiple_of(pair * 2 * cap, 2 * cap)
        hot = hot_slots(pos_ref[...], first, 2 * cap)
        got = dot_tn(recv[pl.ds(first, 2 * cap), :], hot)

        @pl.when(step == 0)
        def _():
            x_acc[...] = got

        @pl.when(step > 0)
        def _():
            x_acc[...] += got

        return carry

    lax.fori_loop(0, n // 2, place, 0)

    def told(j, carry):
        back_request_arrival(j).wait_recv()
        return carry

    lax.fori_loop(1, n, told, 0)
    share(core).start()
    x_t[...] = x_acc[...].astype(BF16)

    xf = x_acc[...]
    scale = lax.rsqrt(jnp.mean(xf * xf, axis=0, keepdims=True) + EPSILON)
    a = (xf * scale * g1_col).astype(BF16)
    a_t[...] = a
    out = dot_nn(wqkv_t[...], a)
    qkv_t[0:hd, :] = out[:hd].astype(BF16) * jnp.array(1.0 / math.sqrt(DH), BF16)
    qkv_t[hd:, :] = out[hd:].astype(BF16)
    kv[...] = dot_nn(a.T, wqkv[:, hd:]).astype(BF16)

    rows = [slice(p * 2 * DH, (p + 1) * 2 * DH) for p in range(pairs)]
    krows = [slice(hd + p * 2 * DH, hd + (p + 1) * 2 * DH) for p in range(pairs)]
    vrows = [slice(2 * hd + p * 2 * DH, 2 * hd + (p + 1) * 2 * DH) for p in range(pairs)]
    jobs = [(i, p) for i in range(group) for p in range(pairs)]

    def members(g):
        return [pl.ds(pl.multiple_of((g * group + i) * length, length), length) for i in range(group)]

    def attend(g, carry):
        parts = members(g)
        key_id = lax.broadcasted_iota(jnp.int32, (length, 2 * length), 0)
        visible = [key_id < lens[0, g * group + i] for i in range(group)]
        scores = [
            dot_nn(kv[parts[i], rows[p]], split_pair(qkv_t[rows[p], parts[i]])) for i, p in jobs
        ]
        probs = []
        for (i, p), score in zip(jobs, scores):
            score = jnp.where(visible[i], score + bias[p], -1000000000.0)
            expo = jnp.exp(score - jnp.max(score, axis=0, keepdims=True))
            prob = expo * (1.0 / jnp.sum(expo, axis=0, keepdims=True))
            p_s[g * group + i, p] = prob
            probs.append(prob.astype(BF16))
        for (i, p), prob in zip(jobs, probs):
            mixed = dot_nn(qkv_t[vrows[p], parts[i]], prob)
            o_t[rows[p], parts[i]] = jnp.concatenate(
                [mixed[:DH, :length], mixed[DH:, length:]], axis=0
            ).astype(BF16)
        return carry

    lax.fori_loop(0, seqs // group, attend, 0)

    m = x_t[...].astype(F32) + dot_nn(wo_t[...], o_t[...])
    scale = lax.rsqrt(jnp.mean(m * m, axis=0, keepdims=True) + EPSILON)
    z = m * scale
    normed = (z * g2_col).astype(BF16)
    c_t[...] = normed
    value, slope = gelu_parts(dot_nn(win_t[...], normed))
    act = value.astype(BF16)
    act_t[...] = act
    du = (dot_nn(wout[...], dy_t[...]) * slope).astype(BF16)
    du_t[...] = du
    y = m + dot_nn(wout_t[...], act)
    for s in range(seqs):
        y_out[s] = y[:, s * length : (s + 1) * length].T.astype(BF16)
    flushes = [
        pltpu.make_async_copy(src, dst, out_sem.at[k])
        for k, (src, dst) in enumerate(
            (
                (y_out, y_far), (ig_out, ig_far), (asked_out, asked_far), (early_tot, early_far),
                (late_tot, late_far), (small_tot, small_far),
            )
        )
    ]
    flushes[0].start()
    dc = dot_nn(win[...], du)
    gain_two = dc * z
    gain_two = sum(gain_two[:, s * length : (s + 1) * length] for s in range(seqs))
    small_tot[1:2, :] = jnp.sum(gain_two.T, axis=0, keepdims=True)
    e = dc * g2_col
    dm = dy_t[...].astype(F32) + scale * (e - z * jnp.mean(e * z, axis=0, keepdims=True))
    dm_t[...] = dm
    dmb = dm.astype(BF16)
    dmb_t[...] = dmb
    do_t[...] = dot_nn(wo[...], dmb).astype(BF16)

    for k in range(ff // width):
        at = slice(k * width, (k + 1) * width)
        early[at, :] = dot_nt(c_t[...], du_t[at, :]).astype(BF16)
    early[ff : 2 * ff, :] = dot_nt(act_t[...], dy_t[...]).astype(BF16)
    if early.shape[0] > 2 * ff:
        early[2 * ff :, :] = jnp.zeros((early.shape[0] - 2 * ff, width), BF16)
    early_sum.start()

    def attend_back(g):
        parts = members(g)
        do2s = [split_pair(do_t[rows[p], parts[i]]) for i, p in jobs]
        dprobs = [dot_nn(kv[parts[i], krows[p]], do2) for (i, p), do2 in zip(jobs, do2s)]
        lows = []
        for (i, p), dprob in zip(jobs, dprobs):
            prob = p_s[g * group + i, p]
            ds = prob * (dprob - jnp.sum(dprob * prob, axis=0, keepdims=True))
            dsum[p] += ds
            lows.append(ds.astype(BF16))
        for (i, p), do2 in zip(jobs, do2s):
            prob = p_s[g * group + i, p].astype(BF16)
            dqkv_t[vrows[p], parts[i]] = dot_nt(do2, prob).astype(BF16)
        for (i, p), low in zip(jobs, lows):
            q2 = split_pair(qkv_t[rows[p], parts[i]])
            dqkv_t[krows[p], parts[i]] = dot_nt(q2, low).astype(BF16)
        for (i, p), low in zip(jobs, lows):
            dq = dot_nn(qkv_t[krows[p], parts[i]], low) * (1.0 / math.sqrt(DH))
            dqkv_t[rows[p], parts[i]] = jnp.concatenate(
                [dq[:DH, :length], dq[DH:, length:]], axis=0
            ).astype(BF16)

    groups = seqs // group

    def back_loop(g, carry):
        attend_back(g)

        @pl.when(g == 0)
        def _():
            early_sum.core_to_lo()

        return carry

    lax.fori_loop(0, groups, back_loop, 0)

    xf = x_t[...].astype(F32)
    scale = lax.rsqrt(jnp.mean(xf * xf, axis=0, keepdims=True) + EPSILON)
    z = xf * scale
    da = dot_nn(wqkv[...], dqkv_t[...])
    gain_one = da * z
    gain_one = sum(gain_one[:, s * length : (s + 1) * length] for s in range(seqs))
    e = da * g1_col
    ig = dm_t[...] + scale * (e - z * jnp.mean(e * z, axis=0, keepdims=True))
    igb_t[...] = ig.astype(BF16)

    def grad_copy(j):
        back = lax.rem(n - j, n)
        return remote(
            slots.at[slot_block(j)], inc.at[core, slot_block(back)],
            grad_send.at[j], grad_recv.at[back], peer(j),
        )

    def grad_arrival(j):
        return remote(
            slots.at[slot_block(j)], inc.at[core, slot_block(j)],
            grad_send.at[j], grad_recv.at[j], peer(j),
        )

    def forward(j, which):
        ref = inc.at[which, slot_block(j)]
        return remote(ref, ref, fwd_send.at[j], fwd_recv.at[j], {"dp": 1 - core})

    def to_slots(k, carry):
        first = pl.multiple_of(k * wide_slots, wide_slots)
        slots[pl.ds(first, wide_slots), :] = dot_nt(
            hot_slots(back_pos[...], first, wide_slots), igb_t[...]
        ).astype(BF16)

        def go(j, inner):
            grad_copy(j).start()
            return inner

        owners = wide_slots // cap
        lax.fori_loop(jnp.maximum(k * owners, 1), (k + 1) * owners, go, 0)
        return carry

    steps = slots.shape[0] // wide_slots

    def send_rows(first, last):
        lax.fori_loop(first * steps // 8, last * steps // 8, to_slots, 0)

    for k in range(3 * hd // width):
        at = slice(k * width, (k + 1) * width)
        late[at, :] = dot_nt(a_t[...], dqkv_t[at, :]).astype(BF16)
    late[3 * hd : 4 * hd, :] = dot_nt(o_t[...], dmb_t[...]).astype(BF16)
    if late.shape[0] > 4 * hd:
        late[4 * hd :, :] = jnp.zeros((late.shape[0] - 4 * hd, width), BF16)
    late_sum.start()

    def pass_on(step, carry):
        j = n - 1 - step
        grad_arrival(j).wait_recv()
        forward(j, core).start()
        return carry

    late_sum.core_to_lo()
    early_sum.lo_to_hi()
    send_rows(0, 3)
    keep = pltpu.make_async_copy(slots.at[slot_block(0)], inc.at[core, slot_block(0)], smem_sem)
    keep.start()
    remote(
        slots.at[slot_block(0)], inc.at[core, slot_block(0)], fwd_send.at[0], fwd_recv.at[0],
        {"dp": 1 - core},
    ).start()
    def bias_back(r, carry):
        part = pl.ds(pl.multiple_of(r * 8, 8), 8)
        bt = buck_t[part, :]
        grads = [dsum[h // 2, part, (h % 2) * length : (h % 2 + 1) * length] for h in range(heads)]
        for b in range(bucket_count):
            here = bt == float(b)
            for h in range(heads):
                b_acc[h, b] += jnp.where(here, grads[h], 0.0)
        return carry

    lax.fori_loop(0, length // 8, bias_back, 0)
    small_parts = [jnp.sum(gain_one.T, axis=0, keepdims=True), small_tot[1:2, :]]
    for h in range(heads):
        by_bucket = jnp.sum(b_acc[h], axis=1)
        row = jnp.sum(by_bucket.T, axis=0, keepdims=True)
        small_parts.append(
            jnp.concatenate([row, jnp.zeros((1, LANES - bucket_count), F32)], axis=1)
        )
    small_sum.start(jnp.concatenate(small_parts, axis=0))
    late_sum.lo_to_hi()
    small_sum.core_to_lo()
    early_sum.hi_to_gather()
    late_sum.hi_to_gather()
    small_sum.lo_to_hi()
    send_rows(3, 6)
    early_sum.gather_to_lo()
    late_sum.gather_to_lo()
    send_rows(6, 8)
    for s in range(seqs):
        ig_out[s] = ig[:, s * length : (s + 1) * length].T
    flushes[1].start()
    early_sum.gather_to_core()
    late_sum.gather_to_core()
    lax.fori_loop(0, 15, pass_on, 0)
    small_sum.finish()
    flushes[5].start()
    early_sum.finish()
    flushes[3].start()
    late_sum.finish()
    flushes[4].start()
    share(core).wait_send()
    share(1 - core).wait_recv()
    flushes[2].start()
    keep.wait()

    def rows_in(j, carry):
        forward(j, 1 - core).wait_recv()
        forward(j, core).wait_send()
        return carry

    lax.fori_loop(0, n, rows_in, 0)

    def sent(j, carry):
        request(j).wait_send()
        back_request(j).wait_send()
        row_copy(j).wait_send()
        grad_copy(j).wait_send()
        return carry

    lax.fori_loop(1, n, sent, 0)
    for flush in flushes:
        flush.wait()


def step_kernel(n, lo, cap, used, sizes, *refs):
    parts, at = [], 0
    for size in sizes:
        parts.append(refs[at : at + size])
        at += size
    step_body(n, lo, cap, used, *parts)


def scatter_body(
    n, cap, used, asked_far, counts, inc, early, late, small, y_in, ig_in,
    y_out, ig_out, grad, g1, wq, wk, wv, wo, bias, g2, win, wout,
    acc, wide, zero, inc_v, y_v, ig_v, early_v, late_v, wq_v, wk_v, wv_v, wo_v, win_v, wout_v,
    out_sem, in_sem, pass_sem, asked, asked_sem,
):
    rows_dev, width = grad.shape
    chunk = zero.shape[0]
    domain_rows = used // 3
    per_domain = domain_rows // chunk
    slots = n * cap
    hd = wq.shape[1]
    ff = win.shape[1]
    loads = [
        pltpu.make_async_copy(src, dst, in_sem.at[k])
        for k, (src, dst) in enumerate(
            ((inc, inc_v), (early, early_v), (late, late_v), (y_in, y_v), (ig_in, ig_v))
        )
    ]
    ask = pltpu.make_async_copy(asked_far, asked, asked_sem)
    ask.start()
    loads[0].start()
    zero[...] = jnp.zeros_like(zero)

    def chunk_at(k):
        return pl.ds(pl.multiple_of(k * chunk, chunk), chunk)

    def clear_copy(k):
        return pltpu.make_async_copy(zero, grad.at[chunk_at(k)], out_sem.at[k])

    def out_copy(k):
        return pltpu.make_async_copy(acc.at[chunk_at(k)], grad.at[chunk_at(k)], out_sem.at[k])

    def in_use(k):
        return (k % per_domain) * chunk < counts[k // per_domain]

    def spare(k, carry):
        clear_copy(k).start()
        return carry

    def prepare(k, carry):
        @pl.when(in_use(k))
        def _():
            def clear(r, inner):
                at = pl.multiple_of(k * chunk + r * 256, 256)
                acc[pl.ds(at, 256), :] = jnp.zeros((256, width), F32)
                return inner

            lax.fori_loop(0, chunk // 256, clear, 0)

        return carry

    lax.fori_loop(0, used // chunk, prepare, 0)
    loads[0].wait()
    for load in loads[1:]:
        load.start()
    lax.fori_loop(used // chunk, rows_dev // chunk, spare, 0)

    def unused(k, carry):
        @pl.when(jnp.logical_not(in_use(k)))
        def _():
            clear_copy(k).start()

        return carry

    lax.fori_loop(0, used // chunk, unused, 0)

    def widen(r, carry):
        at = pl.ds(pl.multiple_of(r * 256, 256), 256)
        wide[at, :] = inc_v[at, :].astype(F32)
        return carry

    lax.fori_loop(0, 2 * slots // 256, widen, 0)

    def source(k, carry):
        base = k * 2 * LANES

        def eight(g, inner):
            first = g * 8
            ats = [asked[base + first + r] for r in range(8)]
            sums = [
                acc[pl.ds(ats[r], 1), :] + wide[pl.ds(k * cap + first + r, 1), :] for r in range(8)
            ]
            for r in range(8):
                acc[pl.ds(ats[r], 1), :] = sums[r]
            return inner

        lax.fori_loop(0, (asked[base + LANES] + 7) // 8, eight, 0)
        return carry

    ask.wait()
    lax.fori_loop(0, 2 * n, source, 0)

    def write(k, carry):
        @pl.when(in_use(k))
        def _():
            out_copy(k).start()

        return carry

    lax.fori_loop(0, used // chunk, write, 0)

    passes = []

    def hand_on(src, dst):
        passes.append(pltpu.make_async_copy(src, dst, pass_sem.at[len(passes)]))
        passes[-1].start()

    for load in loads[1:]:
        load.wait()
    hand_on(y_v, y_out)
    hand_on(ig_v, ig_out)
    for i, (value, out) in enumerate(((wq_v, wq), (wk_v, wk), (wv_v, wv))):
        for k in range(hd // width):
            at = i * hd + k * width
            value[:, k * width : (k + 1) * width] = late_v[at : at + width, :].astype(F32)
        hand_on(value, out)
    wo_v[...] = late_v[3 * hd : 4 * hd, :].astype(F32)
    hand_on(wo_v, wo)
    for k in range(ff // width):
        at = slice(k * width, (k + 1) * width)
        win_v[:, at] = early_v[at, :].astype(F32)
    hand_on(win_v, win)
    wout_v[...] = early_v[ff : 2 * ff, :].astype(F32)
    hand_on(wout_v, wout)
    g1[...] = small[0:1, :]
    g2[...] = small[1:2, :]
    heads, buckets = bias.shape
    bias[...] = small[2 : 2 + heads, 0:buckets]

    def finish(k, carry):
        clear_copy(k).wait()
        return carry

    lax.fori_loop(0, rows_dev // chunk, finish, 0)
    for copy in passes:
        copy.wait()


def on_device(
    hashed_ids, owners, domain_tags, user_counts, lengths, buckets, table, gain_one,
    query_weight_matrix, key_weight_matrix, value_weight_matrix, attention_output_weight,
    bias_table, gain_two, feedforward_input_weight, feedforward_output_weight, cotangent,
):
    n = lax.axis_size("emb")
    seqs, length = hashed_ids.shape
    tokens = seqs * length
    rows_dev, width = table.shape
    used = 3 * (rows_dev // 4)
    cap = max(2, 2 * tokens // n)
    hd = query_weight_matrix.shape[1]
    ff = feedforward_input_weight.shape[1]
    heads = hd // DH
    pairs = heads // 2
    bucket_count = bias_table.shape[0]
    slots = n * cap
    lo = 2 ** ((n.bit_length()) // 2)
    unit = 2 * n * 16
    early_rows = -(-2 * ff // unit) * unit
    late_rows = -(-4 * hd // unit) * unit
    vmem = pl.BlockSpec(memory_space=pltpu.VMEM)
    smem = pl.BlockSpec(memory_space=pltpu.SMEM)
    anywhere = pl.BlockSpec(memory_space=pl.ANY)
    dma = pltpu.SemaphoreType.DMA
    shape = jax.ShapeDtypeStruct

    operands = (
        hashed_ids, owners.reshape(seqs, length), domain_tags, user_counts, lengths, bias_table.T,
        buckets, gain_one.reshape(1, width), gain_two.reshape(1, width), table, cotangent,
        query_weight_matrix, key_weight_matrix, value_weight_matrix, attention_output_weight,
        feedforward_input_weight, feedforward_output_weight,
    )
    results = (
        shape((seqs, length, width), BF16),
        shape((seqs, length, width), F32),
        shape((2, slots, width), BF16),
        shape((2, n, 2, LANES), jnp.int32),
        shape((early_rows, width), BF16),
        shape((late_rows, width), BF16),
        shape((8, LANES), F32),
    )
    lookup_scratch = [
        pltpu.VMEM((n, 1, LANES), jnp.int32),
        pltpu.VMEM((n, 1, LANES), jnp.int32),
        pltpu.SMEM((n, 1, LANES), jnp.int32),
        pltpu.VMEM((used, width), BF16),
        pltpu.VMEM((rows_dev, width), F32),
        pltpu.VMEM((cap, width), F32),
        pltpu.VMEM((slots, width), BF16),
        pltpu.VMEM((slots, width), BF16),
        pltpu.VMEM((width, tokens), F32),
        pltpu.VMEM((seqs, length), jnp.int32),
        pltpu.VMEM((slots, width), BF16),
        pltpu.VMEM((early_rows, width), BF16),
        pltpu.VMEM((late_rows, width), BF16),
        pltpu.VMEM((seqs, length), jnp.int32),
        pltpu.VMEM((n, 2, LANES), jnp.int32),
        dma((n,)), dma((n,)),
        dma((n,)), dma((n,)), dma((n,)), dma((n,)), dma((2,)), dma((6,)), dma,
        dma((n,)), dma((n,)), dma((n,)), dma((n,)),
    ]
    block_scratch = [
        pltpu.VMEM((3 * hd, width), BF16),
        pltpu.VMEM((width, 3 * hd), BF16),
        pltpu.VMEM((width, hd), BF16),
        pltpu.VMEM((ff, width), BF16),
        pltpu.VMEM((width, ff), BF16),
        pltpu.VMEM((length, length), F32),
        pltpu.VMEM((pairs, length, 2 * length), F32),
        pltpu.VMEM((width, tokens), BF16),
        pltpu.VMEM((width, tokens), BF16),
        pltpu.VMEM((3 * hd, tokens), BF16),
        pltpu.VMEM((tokens, 2 * hd), BF16),
        pltpu.VMEM((seqs, pairs, length, 2 * length), F32),
        pltpu.VMEM((hd, tokens), BF16),
        pltpu.VMEM((width, tokens), BF16),
        pltpu.VMEM((ff, tokens), BF16),
        pltpu.VMEM((ff, tokens), BF16),
        pltpu.VMEM((width, tokens), BF16),
        pltpu.VMEM((width, tokens), F32),
        pltpu.VMEM((width, tokens), BF16),
        pltpu.VMEM((hd, tokens), BF16),
        pltpu.VMEM((3 * hd, tokens), BF16),
        pltpu.VMEM((pairs, length, 2 * length), F32),
        pltpu.VMEM((width, tokens), BF16),
        pltpu.VMEM((heads, bucket_count, 8, length), F32),
        pltpu.VMEM((seqs, length, width), BF16),
        pltpu.VMEM((width, hd), BF16),
        pltpu.VMEM((width, hd), BF16),
        pltpu.VMEM((width, hd), BF16),
        pltpu.VMEM((hd, width), BF16),
        pltpu.VMEM((width, ff), BF16),
        pltpu.VMEM((ff, width), BF16),
        dma((11,)),
        pltpu.VMEM((seqs, length), jnp.int32),
        pltpu.VMEM((seqs, length), jnp.int32),
        pltpu.SMEM((seqs,), jnp.int32),
        pltpu.SMEM((user_counts.shape[0],), jnp.int32),
        pltpu.SMEM(lengths.shape, jnp.int32),
        pltpu.SMEM((heads, bucket_count), F32),
        pltpu.VMEM((length, length), jnp.int32),
        pltpu.VMEM((1, width), F32),
        pltpu.VMEM((1, width), F32),
        dma((5,)),
    ]
    block_scratch += [pltpu.VMEM(results[k].shape, results[k].dtype) for k in (0, 1, 3, 4, 5, 6)]
    block_scratch += [dma((6,))]
    early_scratch = Reducer.scratch(n, lo, early_rows)
    late_scratch = Reducer.scratch(n, lo, late_rows)
    small_scratch = SmallReducer.scratch(n, lo)
    scratch = [lookup_scratch, block_scratch, early_scratch, late_scratch, small_scratch]
    sizes = [len(operands), len(results)] + [len(part) for part in scratch]
    y, ig, incoming, asked, early_total, late_total, small_total = pl.pallas_call(
        functools.partial(step_kernel, n, lo, cap, used, sizes),
        out_shape=results,
        in_specs=[anywhere] * len(operands),
        out_specs=(anywhere,) * len(results),
        scratch_shapes=sum(scratch, []),
        compiler_params=pltpu.CompilerParams(
            collective_id=0, has_side_effects=True, vmem_limit_bytes=VMEM_LIMIT
        ),
        name="step",
    )(*operands)

    chunk = math.gcd(1024, used // 3)
    output, input_grad, table_grad, g1, gq, gk, gv, go, gb, g2, gin, gout = pl.pallas_call(
        functools.partial(scatter_body, n, cap, used),
        out_shape=(
            shape((seqs, length, width), BF16),
            shape((seqs, length, width), F32),
            shape((rows_dev, width), F32),
            shape((1, width), F32),
            shape((width, hd), F32),
            shape((width, hd), F32),
            shape((width, hd), F32),
            shape((hd, width), F32),
            shape((heads, bucket_count), F32),
            shape((1, width), F32),
            shape((width, ff), F32),
            shape((ff, width), F32),
        ),
        in_specs=[anywhere, smem, anywhere, anywhere, anywhere, vmem, anywhere, anywhere],
        out_specs=(anywhere,) * 3 + (vmem,) + (anywhere,) * 4 + (vmem,) * 2 + (anywhere,) * 2,
        scratch_shapes=[
            pltpu.VMEM((used + 8, width), F32),
            pltpu.VMEM((2 * slots, width), F32),
            pltpu.VMEM((chunk, width), F32),
            pltpu.VMEM((2 * slots, width), BF16),
            pltpu.VMEM((seqs, length, width), BF16),
            pltpu.VMEM((seqs, length, width), F32),
            pltpu.VMEM((early_rows, width), BF16),
            pltpu.VMEM((late_rows, width), BF16),
            pltpu.VMEM((width, hd), F32),
            pltpu.VMEM((width, hd), F32),
            pltpu.VMEM((width, hd), F32),
            pltpu.VMEM((hd, width), F32),
            pltpu.VMEM((width, ff), F32),
            pltpu.VMEM((ff, width), F32),
            dma((rows_dev // chunk,)), dma((5,)), dma((8,)),
            pltpu.SMEM((2 * n * 2 * LANES,), jnp.int32), dma,
        ],
        compiler_params=pltpu.CompilerParams(vmem_limit_bytes=VMEM_LIMIT),
        name="scatter",
    )(
        asked.reshape(-1), user_counts, incoming.reshape(2 * slots, width), early_total, late_total,
        small_total, y, ig,
    )
    return (
        output, input_grad, table_grad, g1.reshape(width), gq, gk, gv, go, gb.T, g2.reshape(width),
        gin, gout,
    )


def solution(mesh):
    split = ("emb", "dp")
    return jax.shard_map(
        on_device,
        mesh=mesh,
        in_specs=(
            P(split, None), P(split, None, None), P(split), P(), P(split, None), P(),
            P("emb", None), P(), P(), P(), P(), P(), P(), P(), P(), P(), P(split, None, None),
        ),
        out_specs=(
            P(split, None, None), P(split, None, None), P("emb", None), P(), P(), P(), P(), P(),
            P(), P(), P(), P(),
        ),
        check_vma=False,
    )
```

profile of v0, /device:TPU:27, one launch (start us, length us, event | category | flops | bytes accessed | tf_op | source)
XLA Modules:
  0.0 77.1 jit_solution(7712136703667099132)
XLA Ops:
  0.7 64.7 %step.1 = (bf16[8,128,128]{2,1,0:T(8,128)(2,1)}, f32[8,128,128]{2,1,0:T(8,128)}, bf16[2,2048,128]{2,1,0:T(8,128)(2,1)}, s32[2,16,2,128]{3,2,1,0:T(2,128)}, bf16[...) custom-call(s32[8,128]{1,0:T(8,128)} %refs_0_.1, s32[8,128]{1,0:T(8,128)} %bitcast.11, ...), custom_call_target="tpu_custom_call" | custom-call | tf_op jit(solution)/shard_map/step/pallas_call | solution.py:1160
  65.3 11.8 %scatter.1 = (bf16[8,128,128]{2,1,0:T(8,128)(2,1)}, f32[8,128,128]{2,1,0:T(8,128)}, f32[32768,128]{1,0:T(8,128)}, f32[1,128]{1,0:T(1,128)}, f32[128,384]{1,0:T(8...) custom-call(s32[8192]{0:T(1024)} %bitcast.10, ...), custom_call_target="tpu_custom_call" | custom-call | tf_op jit(solution)/shard_map/scatter/pallas_call | solution.py:1173
where the time goes:
time: 77.8 us; the launch traced here: 77.1 us
  Pallas kernels  76.4 us (98%)
    pallas_call x1, Pallas kernels, on_device(): pl.pallas_call(functools.partial(step_kernel, n, lo, cap, used, sizes), o...  64.7 us
    pallas_call x1, Pallas kernels, on_device(): pl.pallas_call(functools.partial(scatter_body, n, cap, used), out_shape=(...  11.8 us

commit v1 on v0

--- a/solution.py
+++ b/solution.py
@@ -308,13 +308,13 @@
 
 
 def step_body(
-    n, lo, cap, used, refs_in, refs_out, lookup_refs, block_refs, early_refs, late_refs, small_refs,
+    n, lo, cap, gcap, used, refs_in, refs_out, lookup_refs, block_refs, early_refs, late_refs, small_refs,
 ):
     (
         ids_far, own_far, tags_far, counts_far, lens_far, btab_far, buckets_far, g1_far, g2_far,
         table, *far,
     ) = refs_in
-    y_far, ig_far, inc, asked_far, early_far, late_far, small_far = refs_out
+    y_far, ig_far, inc, asked_far, early_far, late_far, small_far, over, excess = refs_out
     (
         req, asked_v, asked_s, tab_low, tab, gbuf, send, recv, x_acc, pos_ref, slots, early, late,
         back_pos, back_req, back_send, back_recv,
@@ -344,7 +344,9 @@
     pieces = tab_sem.shape[0]
     piece = used // pieces
     group = 4
-    wide_slots = 256
+    owners_at_once = max(1, 256 // cap)
+    wide_slots = owners_at_once * gcap
+    ocap = cap - gcap
     early_sum = Reducer(n, lo, me, core, early, early_tot, early_refs)
     late_sum = Reducer(n, lo, me, core, late, late_tot, late_refs)
     small_sum = SmallReducer(n, lo, me, core, small_tot, small_refs)
@@ -541,7 +543,10 @@
             at = jnp.maximum(at, jnp.where(key_cols[e] == key[s : s + 1, :], first_cols[e], 0.0))
         found.append(jnp.max(at, axis=0, keepdims=True))
     found = jnp.concatenate(found, axis=0).astype(jnp.int32) - 1
-    back_pos[...] = jnp.where(live, rel * cap + found, -1)
+    back_at = rel * gcap + found
+    if ocap:
+        back_at = jnp.where(found < gcap, back_at, n * gcap + rel * ocap + found - gcap)
+    back_pos[...] = jnp.where(live, back_at, -1)
     below = used - local
     low = (below & 255).astype(F32)
     high = lax.shift_right_logical(below, 8).astype(F32)
@@ -553,7 +558,9 @@
         slot_hot = jnp.where(slot_id == firsts[s].astype(jnp.int32), 1.0, 0.0).astype(BF16)
         asking = asking + dot_nt(values.astype(BF16), slot_hot)
     wanted = used - (asking[:n] * 256.0 + asking[n:]).astype(jnp.int32)
-    limits = jnp.broadcast_to(running, (n, LANES)).astype(jnp.int32)
+    lane = lax.broadcasted_iota(jnp.int32, (n, LANES), 1)
+    largest = jnp.max(running, axis=0, keepdims=True)
+    limits = jnp.where(lane == 0, running, largest).astype(jnp.int32)
     for j in range(n):
         back_req[j, 0:1] = wanted[j : j + 1, :]
         back_req[j, 1:2] = limits[j : j + 1, :]
@@ -774,21 +781,24 @@
     ig = dm_t[...] + scale * (e - z * jnp.mean(e * z, axis=0, keepdims=True))
     igb_t[...] = ig.astype(BF16)
 
+    def grad_block(j):
+        return pl.ds(pl.multiple_of(j * gcap, gcap), gcap)
+
     def grad_copy(j):
         back = lax.rem(n - j, n)
         return remote(
-            slots.at[slot_block(j)], inc.at[core, slot_block(back)],
+            slots.at[grad_block(j)], inc.at[core, grad_block(back)],
             grad_send.at[j], grad_recv.at[back], peer(j),
         )
 
     def grad_arrival(j):
         return remote(
-            slots.at[slot_block(j)], inc.at[core, slot_block(j)],
+            slots.at[grad_block(j)], inc.at[core, grad_block(j)],
             grad_send.at[j], grad_recv.at[j], peer(j),
         )
 
     def forward(j, which):
-        ref = inc.at[which, slot_block(j)]
+        ref = inc.at[which, grad_block(j)]
         return remote(ref, ref, fwd_send.at[j], fwd_recv.at[j], {"dp": 1 - core})
 
     def to_slots(k, carry):
@@ -801,11 +811,11 @@
             grad_copy(j).start()
             return inner
 
-        owners = wide_slots // cap
+        owners = owners_at_once
         lax.fori_loop(jnp.maximum(k * owners, 1), (k + 1) * owners, go, 0)
         return carry
 
-    steps = slots.shape[0] // wide_slots
+    steps = n // owners_at_once
 
     def send_rows(first, last):
         lax.fori_loop(first * steps // 8, last * steps // 8, to_slots, 0)
@@ -827,10 +837,10 @@
     late_sum.core_to_lo()
     early_sum.lo_to_hi()
     send_rows(0, 3)
-    keep = pltpu.make_async_copy(slots.at[slot_block(0)], inc.at[core, slot_block(0)], smem_sem)
+    keep = pltpu.make_async_copy(slots.at[grad_block(0)], inc.at[core, grad_block(0)], smem_sem)
     keep.start()
     remote(
-        slots.at[slot_block(0)], inc.at[core, slot_block(0)], fwd_send.at[0], fwd_recv.at[0],
+        slots.at[grad_block(0)], inc.at[core, grad_block(0)], fwd_send.at[0], fwd_recv.at[0],
         {"dp": 1 - core},
     ).start()
     def bias_back(r, carry):
@@ -864,6 +874,18 @@
     for s in range(seqs):
         ig_out[s] = ig[:, s * length : (s + 1) * length].T
     flushes[1].start()
+    if ocap:
+        for k in range(n * ocap // 256):
+            first = n * gcap + k * 256
+            slots[pl.ds(first, 256), :] = dot_nt(
+                hot_slots(back_pos[...], first, 256), igb_t[...]
+            ).astype(BF16)
+        over_rows = pl.ds(0, n * ocap)
+        spill = pltpu.make_async_copy(
+            slots.at[pl.ds(n * gcap, n * ocap)], over.at[over_rows], smem_sem
+        )
+        keep.wait()
+        spill.start()
     early_sum.gather_to_core()
     late_sum.gather_to_core()
     lax.fori_loop(0, 15, pass_on, 0)
@@ -876,7 +898,20 @@
     share(core).wait_send()
     share(1 - core).wait_recv()
     flushes[2].start()
-    keep.wait()
+    if ocap:
+        spill.wait()
+        most = jnp.zeros((1, LANES), F32)
+
+        def peak(j, most):
+            return jnp.maximum(
+                most, jnp.maximum(asked_out[0, j, 1:2], asked_out[1, j, 1:2]).astype(F32)
+            )
+
+        most = lax.fori_loop(0, n, peak, most)
+        excess[0, 0] = jnp.max(most).astype(jnp.int32)
+    else:
+        keep.wait()
+        excess[0, 0] = 0
 
     def rows_in(j, carry):
         forward(j, 1 - core).wait_recv()
@@ -897,19 +932,99 @@
         flush.wait()
 
 
-def step_kernel(n, lo, cap, used, sizes, *refs):
+def step_kernel(n, lo, cap, gcap, used, sizes, *refs):
     parts, at = [], 0
     for size in sizes:
         parts.append(refs[at : at + size])
         at += size
-    step_body(n, lo, cap, used, *parts)
+    step_body(n, lo, cap, gcap, used, *parts)
+
+
+def rest_body(n, rows, mine, out, send_sem, recv_sem, fwd_send, fwd_recv, self_sem):
+    me = lax.axis_index("emb")
+    core = lax.axis_index("dp")
+    barrier = pltpu.get_barrier_semaphore()
+
+    def peer(j):
+        return {"emb": lax.rem(me + j, n)}
+
+    def greet(k, carry):
+        pl.semaphore_signal(barrier, inc=1, device_id=peer(k), device_id_type=MESH)
+        return carry
+
+    lax.fori_loop(1, n, greet, 0)
+    pl.semaphore_signal(barrier, inc=1, device_id={"dp": 1 - core}, device_id_type=MESH)
+    pl.semaphore_wait(barrier, n)
+
+    def block(j):
+        return pl.ds(pl.multiple_of(j * rows, rows), rows)
+
+    def landed(which, j):
+        return out.at[pl.ds(pl.multiple_of((which * n + j) * rows, rows), rows)]
+
+    def copy(j):
+        back = lax.rem(n - j, n)
+        return remote(
+            mine.at[block(j)], landed(core, back), send_sem.at[j], recv_sem.at[back], peer(j)
+        )
+
+    def arrival(j):
+        return remote(mine.at[block(j)], landed(core, j), send_sem.at[j], recv_sem.at[j], peer(j))
+
+    def forward(j, which):
+        ref = landed(which, j)
+        return remote(ref, ref, fwd_send.at[j], fwd_recv.at[j], {"dp": 1 - core})
+
+    def start(j, carry):
+        copy(j).start()
+        return carry
+
+    lax.fori_loop(1, n, start, 0)
+    keep = pltpu.make_async_copy(mine.at[block(0)], landed(core, 0), self_sem)
+    keep.start()
+    keep.wait()
+    forward(0, core).start()
+
+    def pass_on(j, carry):
+        arrival(j).wait_recv()
+        forward(j, core).start()
+        return carry
+
+    lax.fori_loop(1, n, pass_on, 0)
+
+    def finish(j, carry):
+        forward(j, core).wait_send()
+        forward(j, 1 - core).wait_recv()
+        return carry
+
+    lax.fori_loop(0, n, finish, 0)
+
+    def sent(j, carry):
+        copy(j).wait_send()
+        return carry
+
+    lax.fori_loop(1, n, sent, 0)
+
+
+def exchange_rest(n, rows, over):
+    dma = pltpu.SemaphoreType.DMA
+    anywhere = pl.BlockSpec(memory_space=pl.ANY)
+    return pl.pallas_call(
+        functools.partial(rest_body, n, rows),
+        out_shape=jax.ShapeDtypeStruct(over.shape, over.dtype),
+        in_specs=[anywhere],
+        out_specs=anywhere,
+        scratch_shapes=[dma((n,)), dma((n,)), dma((n,)), dma((n,)), dma],
+        compiler_params=pltpu.CompilerParams(collective_id=1, has_side_effects=True),
+        name="rest",
+    )(over)
 
 
 def scatter_body(
-    n, cap, used, asked_far, counts, inc, early, late, small, y_in, ig_in,
+    n, cap, rest, used, asked_far, counts, inc, over, early, late, small, y_in, ig_in,
     y_out, ig_out, grad, g1, wq, wk, wv, wo, bias, g2, win, wout,
-    acc, wide, zero, inc_v, y_v, ig_v, early_v, late_v, wq_v, wk_v, wv_v, wo_v, win_v, wout_v,
-    out_sem, in_sem, pass_sem, asked, asked_sem,
+    acc, wide, zero, inc_v, over_v, y_v, ig_v, early_v, late_v, wq_v, wk_v, wv_v, wo_v, win_v, wout_v,
+    out_sem, in_sem, pass_sem, asked, asked_sem, spare_rows,
 ):
     rows_dev, width = grad.shape
     chunk = zero.shape[0]
@@ -921,7 +1036,10 @@
     loads = [
         pltpu.make_async_copy(src, dst, in_sem.at[k])
         for k, (src, dst) in enumerate(
-            ((inc, inc_v), (early, early_v), (late, late_v), (y_in, y_v), (ig_in, ig_v))
+            (
+                (inc, inc_v), (over, over_v), (early, early_v), (late, late_v), (y_in, y_v),
+                (ig_in, ig_v),
+            )
         )
     ]
     ask = pltpu.make_async_copy(asked_far, asked, asked_sem)
@@ -961,6 +1079,7 @@
     loads[0].wait()
     for load in loads[1:]:
         load.start()
+    loads[1].wait()
     lax.fori_loop(used // chunk, rows_dev // chunk, spare, 0)
 
     def unused(k, carry):
@@ -992,7 +1111,25 @@
                 acc[pl.ds(ats[r], 1), :] = sums[r]
             return inner
 
-        lax.fori_loop(0, (asked[base + LANES] + 7) // 8, eight, 0)
+        count = asked[base + LANES]
+        lax.fori_loop(0, (jnp.minimum(count, cap) + 7) // 8, eight, 0)
+        if rest:
+            def more(g, inner):
+                first = g * 8
+                ats = [asked[base + cap + first + r] for r in range(8)]
+                rows = [
+                    over_v[pl.ds(pl.multiple_of(k * rest + first // 16 * 16, 16), 16), :]
+                ][0].astype(F32)
+                spare_rows[...] = rows
+                sums = [
+                    acc[pl.ds(ats[r], 1), :] + spare_rows[pl.ds(first % 16 + r, 1), :]
+                    for r in range(8)
+                ]
+                for r in range(8):
+                    acc[pl.ds(ats[r], 1), :] = sums[r]
+                return inner
+
+            lax.fori_loop(0, (jnp.maximum(count - cap, 0) + 7) // 8, more, 0)
         return carry
 
     ask.wait()
@@ -1013,7 +1150,7 @@
         passes.append(pltpu.make_async_copy(src, dst, pass_sem.at[len(passes)]))
         passes[-1].start()
 
-    for load in loads[1:]:
+    for load in loads[2:]:
         load.wait()
     hand_on(y_v, y_out)
     hand_on(ig_v, ig_out)
@@ -1061,6 +1198,8 @@
     pairs = heads // 2
     bucket_count = bias_table.shape[0]
     slots = n * cap
+    gcap = max(16, 3 * cap // 4 // 16 * 16)
+    ocap = cap - gcap
     lo = 2 ** ((n.bit_length()) // 2)
     unit = 2 * n * 16
     early_rows = -(-2 * ff // unit) * unit
@@ -1080,11 +1219,13 @@
     results = (
         shape((seqs, length, width), BF16),
         shape((seqs, length, width), F32),
-        shape((2, slots, width), BF16),
+        shape((2, n * gcap, width), BF16),
         shape((2, n, 2, LANES), jnp.int32),
         shape((early_rows, width), BF16),
         shape((late_rows, width), BF16),
         shape((8, LANES), F32),
+        shape((2 * n * max(ocap, 16), width), BF16),
+        shape((1, 1), jnp.int32),
     )
     lookup_scratch = [
         pltpu.VMEM((n, 1, LANES), jnp.int32),
@@ -1157,11 +1298,11 @@
     small_scratch = SmallReducer.scratch(n, lo)
     scratch = [lookup_scratch, block_scratch, early_scratch, late_scratch, small_scratch]
     sizes = [len(operands), len(results)] + [len(part) for part in scratch]
-    y, ig, incoming, asked, early_total, late_total, small_total = pl.pallas_call(
-        functools.partial(step_kernel, n, lo, cap, used, sizes),
+    y, ig, incoming, asked, early_total, late_total, small_total, over, excess = pl.pallas_call(
+        functools.partial(step_kernel, n, lo, cap, gcap, used, sizes),
         out_shape=results,
         in_specs=[anywhere] * len(operands),
-        out_specs=(anywhere,) * len(results),
+        out_specs=(anywhere,) * (len(results) - 1) + (smem,),
         scratch_shapes=sum(scratch, []),
         compiler_params=pltpu.CompilerParams(
             collective_id=0, has_side_effects=True, vmem_limit_bytes=VMEM_LIMIT
@@ -1169,9 +1310,14 @@
         name="step",
     )(*operands)
 
+    if ocap:
+        over = lax.cond(
+            excess[0, 0] > gcap, functools.partial(exchange_rest, n, ocap), lambda rows: rows, over
+        )
+
     chunk = math.gcd(1024, used // 3)
     output, input_grad, table_grad, g1, gq, gk, gv, go, gb, g2, gin, gout = pl.pallas_call(
-        functools.partial(scatter_body, n, cap, used),
+        functools.partial(scatter_body, n, gcap, ocap, used),
         out_shape=(
             shape((seqs, length, width), BF16),
             shape((seqs, length, width), F32),
@@ -1186,13 +1332,14 @@
             shape((width, ff), F32),
             shape((ff, width), F32),
         ),
-        in_specs=[anywhere, smem, anywhere, anywhere, anywhere, vmem, anywhere, anywhere],
+        in_specs=[anywhere, smem, anywhere, anywhere, anywhere, anywhere, vmem, anywhere, anywhere],
         out_specs=(anywhere,) * 3 + (vmem,) + (anywhere,) * 4 + (vmem,) * 2 + (anywhere,) * 2,
         scratch_shapes=[
             pltpu.VMEM((used + 8, width), F32),
-            pltpu.VMEM((2 * slots, width), F32),
+            pltpu.VMEM((2 * n * gcap, width), F32),
             pltpu.VMEM((chunk, width), F32),
-            pltpu.VMEM((2 * slots, width), BF16),
+            pltpu.VMEM((2 * n * gcap, width), BF16),
+            pltpu.VMEM(over.shape, BF16),
             pltpu.VMEM((seqs, length, width), BF16),
             pltpu.VMEM((seqs, length, width), F32),
             pltpu.VMEM((early_rows, width), BF16),
@@ -1203,14 +1350,14 @@
             pltpu.VMEM((hd, width), F32),
             pltpu.VMEM((width, ff), F32),
             pltpu.VMEM((ff, width), F32),
-            dma((rows_dev // chunk,)), dma((5,)), dma((8,)),
-            pltpu.SMEM((2 * n * 2 * LANES,), jnp.int32), dma,
+            dma((rows_dev // chunk,)), dma((6,)), dma((8,)),
+            pltpu.SMEM((2 * n * 2 * LANES,), jnp.int32), dma, pltpu.VMEM((16, width), F32),
         ],
         compiler_params=pltpu.CompilerParams(vmem_limit_bytes=VMEM_LIMIT),
         name="scatter",
     )(
-        asked.reshape(-1), user_counts, incoming.reshape(2 * slots, width), early_total, late_total,
-        small_total, y, ig,
+        asked.reshape(-1), user_counts, incoming.reshape(2 * n * gcap, width), over, early_total,
+        late_total, small_total, y, ig,
     )
     return (
         output, input_grad, table_grad, g1.reshape(width), gq, gk, gv, go, gb.T, g2.reshape(width),

time: 77.8 us -> 77.4 us (level)
  the two profiles are of different devices: /device:TPU:27 before, /device:TPU:3 now
where the time goes in v1:
time: 77.4 us; the launch traced here: 76.2 us
  Pallas kernels  75 us (97%)
  between operations  1.24 us (2%)
    pallas_call x1, Pallas kernels, on_device(): pl.pallas_call(functools.partial(step_kernel, n, lo, cap, gcap, used, siz...  63.3 us
    pallas_call x1, Pallas kernels, on_device(): pl.pallas_call(functools.partial(scatter_body, n, gcap, ocap, used), out_...  11.7 us

profile of v1, /device:TPU:3, one launch (start us, length us, event | category | flops | bytes accessed | tf_op | source)
XLA Modules:
  0.0 76.2 jit_solution(17997151416908408449)
XLA Ops:
  0.7 63.3 %step.1 = (bf16[8,128,128]{2,1,0:T(8,128)(2,1)}, f32[8,128,128]{2,1,0:T(8,128)}, bf16[2,1536,128]{2,1,0:T(8,128)(2,1)}, s32[2,16,2,128]{3,2,1,0:T(2,128)}, bf16[...) custom-call(s32[8,128]{1,0:T(8,128)} %refs_0_.1, ...), custom_call_target="tpu_custom_call" | custom-call | tf_op jit(solution)/shard_map/step/pallas_call | solution.py:1301
  64.5 11.7 %scatter.1 = (bf16[8,128,128]{2,1,0:T(8,128)(2,1)}, f32[8,128,128]{2,1,0:T(8,128)}, f32[32768,128]{1,0:T(8,128)}, f32[1,128]{1,0:T(1,128)}, f32[128,384]{1,0:T(8...) custom-call(s32[8192]{0:T(1024)} %bitcast.11, ...), custom_call_target="tpu_custom_call" | custom-call | tf_op jit(solution)/shard_map/scatter/pallas_call | solution.py:1319
  (1 shorter events, 0.0 us)

commit v2 on v1

--- a/solution.py
+++ b/solution.py
@@ -646,12 +646,6 @@
 
     lax.fori_loop(0, n // 2, place, 0)
 
-    def told(j, carry):
-        back_request_arrival(j).wait_recv()
-        return carry
-
-    lax.fori_loop(1, n, told, 0)
-    share(core).start()
     x_t[...] = x_acc[...].astype(BF16)
 
     xf = x_acc[...]
@@ -693,6 +687,13 @@
         return carry
 
     lax.fori_loop(0, seqs // group, attend, 0)
+
+    def told(j, carry):
+        back_request_arrival(j).wait_recv()
+        return carry
+
+    lax.fori_loop(1, n, told, 0)
+    share(core).start()
 
     m = x_t[...].astype(F32) + dot_nn(wo_t[...], o_t[...])
     scale = lax.rsqrt(jnp.mean(m * m, axis=0, keepdims=True) + EPSILON)

time: 77.4 us -> 76.8 us (level)
  the two profiles are of different devices: /device:TPU:3 before, /device:TPU:27 now
where the time goes in v2:
time: 76.8 us; the launch traced here: 76 us
  Pallas kernels  74.8 us (97%)
  between operations  1.24 us (2%)
    pallas_call x1, Pallas kernels, on_device(): pl.pallas_call(functools.partial(step_kernel, n, lo, cap, gcap, used, siz...  63.6 us
    pallas_call x1, Pallas kernels, on_device(): pl.pallas_call(functools.partial(scatter_body, n, gcap, ocap, used), out_...  11.2 us

profile of v2, /device:TPU:27, one launch (start us, length us, event | category | flops | bytes accessed | tf_op | source)
XLA Modules:
  0.0 76.0 jit_solution(5164848874334373630)
XLA Ops:
  0.7 63.6 %step.1 = (bf16[8,128,128]{2,1,0:T(8,128)(2,1)}, f32[8,128,128]{2,1,0:T(8,128)}, bf16[2,1536,128]{2,1,0:T(8,128)(2,1)}, s32[2,16,2,128]{3,2,1,0:T(2,128)}, bf16[...) custom-call(s32[8,128]{1,0:T(8,128)} %refs_0_.1, ...), custom_call_target="tpu_custom_call" | custom-call | tf_op jit(solution)/shard_map/step/pallas_call | solution.py:1302
  64.9 11.2 %scatter.1 = (bf16[8,128,128]{2,1,0:T(8,128)(2,1)}, f32[8,128,128]{2,1,0:T(8,128)}, f32[32768,128]{1,0:T(8,128)}, f32[1,128]{1,0:T(1,128)}, f32[128,384]{1,0:T(8...) custom-call(s32[8192]{0:T(1024)} %bitcast.11, ...), custom_call_target="tpu_custom_call" | custom-call | tf_op jit(solution)/shard_map/scatter/pallas_call | solution.py:1320
  (1 shorter events, 0.0 us)
